TPU v7x, 32 devices: a whole 2x2x4 slice. The times are simulated.
32 devices in a mesh: group: 2 (over y), expert: 4 (over x, core), dp: 4 (over z).
Axes of the slice: x: 2, y: 2, z: 4, core: 2. Of those that a mesh axis runs over, the one named last changes fastest.
Arguments:
- cotangent: bfloat16 [8192, 7168], P(('group', 'expert', 'dp')), parts along dimension 0, may hold values from -6 to 6
- expert_ids: int32 [8192, 8], P(('group', 'expert', 'dp')), parts along dimension 0, may hold values from 0 to 255, all different within a row; in each aligned block of 128 rows (0 to 127, 128 to 255, ...) at most 8 rows name the same one
- gate_values: float32 [8192, 8], P(('group', 'expert', 'dp')), parts along dimension 0, may hold values from 0.02 to 0.3
- hidden: bfloat16 [8, 4, 4, 2, 8, 1024], P(('group', 'expert'), 'dp'), parts along dimension 0, may hold values from -6 to 6
- down_weight: bfloat16 [4, 1024, 7168], P('expert', None, 'dp'), may hold values from -0.1875 to 0.1875
Outputs:
- fisher: float32 [8, 1024, 7168], P(('group', 'expert'), None, 'dp'), parts along dimension 0
- hidden_grad: bfloat16 [8, 4, 4, 2, 8, 1024], P(('group', 'expert'), 'dp'), parts along dimension 0
There are 2 independent parts, one for each index of `group`. A program takes and returns all parts, laid end to end along the dimension named above; an argument that names none is the same for every part. Nothing has to cross between parts.
Inputs may be any that keep to these rules, and one draw needn't show every extreme that they name: `expert_ids`: each token names 8 different experts. In each aligned block of 128 tokens no expert is named by more than 8 tokens, a bound that some block reaches.
All inputs are finite; a program needn't handle non-finite values.
Results may differ from a plain program's by a relative error of at most 0.0051.
Values may be sent and summed in bfloat16 or wider, within the bound.
A program may use at most 128 MiB of HBM per device.

v0:
```python
import jax
import jax.numpy as jnp
from jax import lax
from jax.sharding import PartitionSpec as P

GROUP = 128


def per_device(cotangent, expert_ids, gate_values, hidden, down_weight):
    experts = lax.axis_size("expert")
    ways = lax.axis_size("dp")
    width = cotangent.shape[1]
    capacity = hidden.shape[4]
    groups_dev = hidden.shape[3]
    hidden_units = hidden.shape[5]
    window = jnp.arange(experts, dtype=jnp.int32)
    match = expert_ids[:, :, None] == window[None, None, :]
    chosen = jnp.any(match, axis=1).astype(jnp.int32).reshape(groups_dev, GROUP, experts)
    weight_sel = jnp.sum(jnp.where(match, gate_values[:, :, None], jnp.float32(0.0)), axis=1)
    weight_sel = weight_sel.reshape(groups_dev, GROUP, experts)
    rank = jnp.cumsum(chosen, axis=1) - 1
    slots = jnp.arange(capacity, dtype=jnp.int32)
    place = (rank[..., None] == slots) & (chosen[..., None] == 1)
    slot_gate = jnp.sum(jnp.where(place, weight_sel[..., None], jnp.float32(0.0)), axis=1)
    token_rows = cotangent.reshape(groups_dev, GROUP, width)
    picked = jnp.einsum(
        "jgec,jgd->ejcd", place.astype(jnp.bfloat16), token_rows, preferred_element_type=jnp.float32
    )
    routed = (picked * jnp.transpose(slot_gate, (1, 0, 2))[..., None]).astype(jnp.bfloat16)
    columns = lax.all_to_all(
        lax.all_to_all(routed[None], "expert", split_axis=1, concat_axis=1, tiled=True),
        "dp",
        split_axis=4,
        concat_axis=0,
        tiled=True,
    )
    flat_cols = columns.reshape(-1, columns.shape[4])
    grad_rows = lax.psum_scatter(
        lax.dot_general(
            flat_cols, down_weight[0], (((1,), (1,)), ((), ())), preferred_element_type=jnp.float32
        ),
        "dp",
        scatter_dimension=0,
        tiled=True,
    )
    hidden_grad = grad_rows.astype(jnp.bfloat16).reshape(hidden.shape)
    shard_width = columns.shape[4]
    empty_fisher = jnp.zeros((hidden_units, shard_width), jnp.float32)
    piece = lax.all_gather(hidden, "dp", axis=1, tiled=True)
    count = piece.shape[1]

    def turn(index, accum):
        source = index // groups_dev
        block = index % groups_dev
        block_h = lax.dynamic_index_in_dim(piece[0], source, 0, keepdims=False)
        block_h = lax.dynamic_index_in_dim(block_h, block, 1, keepdims=False).reshape(
            -1, hidden_units
        )
        block_c = lax.dynamic_index_in_dim(columns, source, 0, keepdims=False)
        block_c = lax.dynamic_index_in_dim(block_c, block, 1, keepdims=False).reshape(
            -1, shard_width
        )
        prod = lax.dot_general(
            block_h, block_c, (((0,), (0,)), ((), ())), preferred_element_type=jnp.float32
        )
        return accum + prod * prod

    fisher_sum = lax.fori_loop(0, count * groups_dev, turn, empty_fisher)
    fisher = (fisher_sum * (1.0 / (ways * groups_dev)))[None]
    return (fisher, hidden_grad)


def solution(mesh):
    in_specs = (
        P(("group", "expert", "dp"), None),
        P(("group", "expert", "dp"), None),
        P(("group", "expert", "dp"), None),
        P(("group", "expert"), "dp", None, None, None, None),
        P("expert", None, "dp"),
    )
    out_specs = (
        P(("group", "expert"), None, "dp"),
        P(("group", "expert"), "dp", None, None, None, None),
    )
    return jax.shard_map(
        per_device, mesh=mesh, in_specs=in_specs, out_specs=out_specs, check_vma=False
    )
```

profile of v0, /device:TPU:0, one launch (start us, length us, event | category | flops | bytes accessed | tf_op | source)
XLA Modules:
  0.0 210.9 jit_solution(8177170741901431970)
XLA Ops:
  7.2 0.7 fusion.10
  7.9 0.1 copy.27
  8.1 0.2 reduce_window_sum.11
  8.3 0.1 copy.28
  8.4 0.7 select_reduce_fusion.1
  9.1 0.1 select_reduce_fusion
  9.2 2.6 %fusion.7 = bf16[1,4,2,8,7168]{4,3,1,2,0:T(8,128)(2,1)S(1)} fusion(bf16[2,128,7168,1]{2,1,3,0:T(8,128)(2,1)} %bitcast.49, f32[4,2,8]{2,0,1:T(4,128)S(1)} %bitcast.55, s32[2,128,4]{1,2,0:T(4,128)S(1)} %copy.28, pred[2,128,4]{1,2,0:T(4,128)(4,1)S(1)} %copy.29), kind=kOutput, calls=%fused_computation.9 | convolution fusion | flops 118374400 | bytes 4592896 | tf_op jit(solution)/shard_map/jgec,jgd->ejcd/dot_general | solution.py:26
  11.8 0.1 copy.30
  11.9 17.1 %all_to_all.23 = bf16[1,4,2,8,7168]{4,3,2,0,1:T(8,128)(2,1)S(1)} all-to-all(bf16[1,4,2,8,7168]{4,3,2,0,1:T(8,128)(2,1)S(1)} %copy.30), channel_id=1, replica_groups=mesh['group'=2,'expert'=4,'dp'=4] {'expert'}, dimensions={1} | all-to-all | bytes 1835008 | tf_op jit(solution)/shard_map/all_to_all | solution.py:31
  29.0 14.6 %copy.31 = bf16[1,4,2,8,7168]{3,1,2,0,4:T(4,128)(2,1)} copy(bf16[1,4,2,8,7168]{4,3,2,0,1:T(8,128)(2,1)S(1)} %all_to_all.23) | data formatting | bytes 1835008 | tf_op jit(solution)/shard_map/all_to_all | solution.py:31
  43.6 0.0 copy-start
  43.6 18.8 %reshape.79 = bf16[4,2,57344]{2,1,0:T(2,128)(2,1)} reshape(bf16[7168,1,2,4,8]{4,3,2,1,0:T(4,128)(2,1)} %bitcast.47) | data formatting | bytes 1835008
  62.4 4.9 %all-to-all-start.1 = ((bf16[4,2,57344]{2,1,0:T(2,128)(2,1)}), bf16[4,2,57344]{2,1,0:T(2,128)(2,1)S(1)}, u32[]{:S(2)}, u32[]{:S(2)}) async-start(bf16[4,2,57344]{2,1,0:T(2,128)(2,1)} %reshape.79), calls=%async_computation.1 | async-start | bytes 1835008 | tf_op jit(solution)/shard_map/all_to_all | solution.py:30
  67.2 0.0 reduce-scatter.2.cloned.1.call-start
  67.2 0.0 copy-done
  67.3 32.4 %all_gather.3 = bf16[1,4,4,2,8,1024]{5,4,3,2,0,1:T(8,128)(2,1)S(1)} all-gather(bf16[1,1,4,2,8,1024]{5,4,3,2,0,1:T(8,128)(2,1)S(1)} %bitcast.53), channel_id=1, replica_groups=mesh['group'=2,'expert'=4,'dp'=4] {'dp'}, dimensions={1}, use_global_device_ids=true | all-gather | bytes 655360 | tf_op jit(solution)/shard_map/all_gather | solution.py:49
  99.7 0.0 all-to-all-done.1
  99.7 19.4 %reshape.80 = bf16[7168,1,2,4,8]{4,3,2,1,0:T(4,128)(2,1)} reshape(bf16[4,2,57344]{2,1,0:T(2,128)(2,1)S(1)} %all-to-all-done.1) | data formatting | bytes 1835008
  119.0 17.1 %copy.32 = bf16[1,4,2,8,4,1792]{5,3,2,1,4,0:T(8,128)(2,1)S(1)} copy(bf16[1,4,2,8,4,1792]{3,1,2,5,4,0:T(4,128)(2,1)} %bitcast.48) | data formatting | bytes 1835008 | tf_op jit(solution)/shard_map/all_to_all | solution.py:30
  136.2 4.2 %fusion.8 = f32[256,1024]{1,0:T(8,128)} fusion(bf16[256,1792]{1,0:T(8,128)(2,1)S(1)} %bitcast.50, bf16[1,1024,1792]{2,1,0:T(8,128)(2,1)} %param.11), kind=kOutput, calls=%fused_computation.11 | convolution fusion | flops 939524096 | bytes 5636096 | tf_op jit(solution)/shard_map/dot_general | solution.py:39
  140.4 0.0 reduce-scatter.2.cloned.1.call-update
  140.4 55.5 %while.17 = (s32[]{:T(128)}, f32[1024,1792]{1,0:T(8,128)}, bf16[1,4,4,2,8,1024]{5,4,3,2,1,0:T(8,128)(2,1)S(1)}, bf16[4,4,2,8,1792]{4,3,2,1,0:T(8,128)(2,1)S(1)},...) while((s32[]{:T(128)}, f32[1024,1792]{1,0:T(8,128)}, ...), condition=%wide.region_5.6_spmd.clone, body=%wide.region_4.5_spmd.clone.sunk | while | flops 122945560 | bytes 14863173 | solution.py:68
  140.4 4.2 %select_add_fusion.2 = f32[1024,1792]{1,0:T(8,128)} fusion(f32[1024,1792]{1,0:T(8,128)} %get-tuple-element.208, pred[]{:T(512)S(6)} %compare.16, bf16[4,4,2,8,1792]{4,3,2,1,0:T(8,128)(2,1)S(1)} %get-tuple-element.220, s32[]{:T(128)S(6)} %select_n.92, s32[]{:T(128)S(6)} %select_n.95, bf16[1,4,4,2,8,1024]{5,4,3,2,1,0:T(8,128)(2,1)S(1)} %get-tuple-element.219), kind=kOutput, calls=%fused_computation.clone.1 | convolution fusion | flops 122945536 | bytes 14862848 | tf_op jit(solution)/shard_map/while/body/eval_jaxpr/dot_general | solution.py:63
  144.6 7.4 %select_add_fusion.2 = f32[1024,1792]{1,0:T(8,128)} fusion(f32[1024,1792]{1,0:T(8,128)} %get-tuple-element.208, pred[]{:T(512)S(6)} %compare.16, bf16[4,4,2,8,1792]{4,3,2,1,0:T(8,128)(2,1)S(1)} %get-tuple-element.220, s32[]{:T(128)S(6)} %select_n.92, s32[]{:T(128)S(6)} %select_n.95, bf16[1,4,4,2,8,1024]{5,4,3,2,1,0:T(8,128)(2,1)S(1)} %get-tuple-element.219), kind=kOutput, calls=%fused_computation.clone.1 | convolution fusion | flops 122945536 | bytes 14862848 | tf_op jit(solution)/shard_map/while/body/eval_jaxpr/dot_general | solution.py:63
  152.1 7.3 %select_add_fusion.2 = f32[1024,1792]{1,0:T(8,128)} fusion(f32[1024,1792]{1,0:T(8,128)} %get-tuple-element.208, pred[]{:T(512)S(6)} %compare.16, bf16[4,4,2,8,1792]{4,3,2,1,0:T(8,128)(2,1)S(1)} %get-tuple-element.220, s32[]{:T(128)S(6)} %select_n.92, s32[]{:T(128)S(6)} %select_n.95, bf16[1,4,4,2,8,1024]{5,4,3,2,1,0:T(8,128)(2,1)S(1)} %get-tuple-element.219), kind=kOutput, calls=%fused_computation.clone.1 | convolution fusion | flops 122945536 | bytes 14862848 | tf_op jit(solution)/shard_map/while/body/eval_jaxpr/dot_general | solution.py:63
  159.4 7.3 %select_add_fusion.2 = f32[1024,1792]{1,0:T(8,128)} fusion(f32[1024,1792]{1,0:T(8,128)} %get-tuple-element.208, pred[]{:T(512)S(6)} %compare.16, bf16[4,4,2,8,1792]{4,3,2,1,0:T(8,128)(2,1)S(1)} %get-tuple-element.220, s32[]{:T(128)S(6)} %select_n.92, s32[]{:T(128)S(6)} %select_n.95, bf16[1,4,4,2,8,1024]{5,4,3,2,1,0:T(8,128)(2,1)S(1)} %get-tuple-element.219), kind=kOutput, calls=%fused_computation.clone.1 | convolution fusion | flops 122945536 | bytes 14862848 | tf_op jit(solution)/shard_map/while/body/eval_jaxpr/dot_general | solution.py:63
  166.7 7.3 %select_add_fusion.2 = f32[1024,1792]{1,0:T(8,128)} fusion(f32[1024,1792]{1,0:T(8,128)} %get-tuple-element.208, pred[]{:T(512)S(6)} %compare.16, bf16[4,4,2,8,1792]{4,3,2,1,0:T(8,128)(2,1)S(1)} %get-tuple-element.220, s32[]{:T(128)S(6)} %select_n.92, s32[]{:T(128)S(6)} %select_n.95, bf16[1,4,4,2,8,1024]{5,4,3,2,1,0:T(8,128)(2,1)S(1)} %get-tuple-element.219), kind=kOutput, calls=%fused_computation.clone.1 | convolution fusion | flops 122945536 | bytes 14862848 | tf_op jit(solution)/shard_map/while/body/eval_jaxpr/dot_general | solution.py:63
  174.0 7.3 %select_add_fusion.2 = f32[1024,1792]{1,0:T(8,128)} fusion(f32[1024,1792]{1,0:T(8,128)} %get-tuple-element.208, pred[]{:T(512)S(6)} %compare.16, bf16[4,4,2,8,1792]{4,3,2,1,0:T(8,128)(2,1)S(1)} %get-tuple-element.220, s32[]{:T(128)S(6)} %select_n.92, s32[]{:T(128)S(6)} %select_n.95, bf16[1,4,4,2,8,1024]{5,4,3,2,1,0:T(8,128)(2,1)S(1)} %get-tuple-element.219), kind=kOutput, calls=%fused_computation.clone.1 | convolution fusion | flops 122945536 | bytes 14862848 | tf_op jit(solution)/shard_map/while/body/eval_jaxpr/dot_general | solution.py:63
  181.3 7.3 %select_add_fusion.2 = f32[1024,1792]{1,0:T(8,128)} fusion(f32[1024,1792]{1,0:T(8,128)} %get-tuple-element.208, pred[]{:T(512)S(6)} %compare.16, bf16[4,4,2,8,1792]{4,3,2,1,0:T(8,128)(2,1)S(1)} %get-tuple-element.220, s32[]{:T(128)S(6)} %select_n.92, s32[]{:T(128)S(6)} %select_n.95, bf16[1,4,4,2,8,1024]{5,4,3,2,1,0:T(8,128)(2,1)S(1)} %get-tuple-element.219), kind=kOutput, calls=%fused_computation.clone.1 | convolution fusion | flops 122945536 | bytes 14862848 | tf_op jit(solution)/shard_map/while/body/eval_jaxpr/dot_general | solution.py:63
  188.6 7.3 %select_add_fusion.2 = f32[1024,1792]{1,0:T(8,128)} fusion(f32[1024,1792]{1,0:T(8,128)} %get-tuple-element.208, pred[]{:T(512)S(6)} %compare.16, bf16[4,4,2,8,1792]{4,3,2,1,0:T(8,128)(2,1)S(1)} %get-tuple-element.220, s32[]{:T(128)S(6)} %select_n.92, s32[]{:T(128)S(6)} %select_n.95, bf16[1,4,4,2,8,1024]{5,4,3,2,1,0:T(8,128)(2,1)S(1)} %get-tuple-element.219), kind=kOutput, calls=%fused_computation.clone.1 | convolution fusion | flops 122945536 | bytes 14862848 | tf_op jit(solution)/shard_map/while/body/eval_jaxpr/dot_general | solution.py:63
  195.9 6.6 %multiply_bitcast_fusion = f32[1,1024,1792]{2,1,0:T(8,128)} fusion(f32[1024,1792]{1,0:T(8,128)} %get-tuple-element.140), kind=kLoop, calls=%fused_computation.10 | loop fusion | flops 1835008 | bytes 14680064 | tf_op jit(solution)/shard_map/broadcast_in_dim | solution.py:69
  202.5 0.0 reduce-scatter.2.cloned.1.call-done
  202.5 1.6 convert_element_type.26
  (6 shorter events, 0.0 us)
Async XLA Ops:
  43.6 23.7 %copy-start = (bf16[1,1,4,2,8,1024]{5,4,3,2,1,0:T(8,128)(2,1)S(1)}, bf16[1,1,4,2,8,1024]{5,4,3,2,1,0:T(8,128)(2,1)}, u32[]{:S(2)}) copy-start(bf16[1,1,4,2,8,1024]{5,4,3,2,1,0:T(8,128)(2,1)} %param.10) | copy-start | bytes 393220
  62.4 37.3 %all-to-all-start.1 = ((bf16[4,2,57344]{2,1,0:T(2,128)(2,1)}), bf16[4,2,57344]{2,1,0:T(2,128)(2,1)S(1)}, u32[]{:S(2)}, u32[]{:S(2)}) async-start(bf16[4,2,57344]{2,1,0:T(2,128)(2,1)} %reshape.79), calls=%async_computation.1 | async-start | bytes 1835008 | tf_op jit(solution)/shard_map/all_to_all | solution.py:30
  67.2 135.2 %reduce-scatter.2.cloned.1.call-start = ((), (), s32[]{:S(2)}) async-start(), calls=%async_computation.3 | async-start | bytes 1310720 | tf_op jit(solution)/shard_map/reduce_scatter | solution.py:38
Sparse Core Ops, SparseCore 0:
  140.5 27.8 reduce-scatter.1
where the time goes:
time: 212 us; the launch traced here: 211 us
  local copies, waits for them, and re-layouts  70.2 us (33%)
  matrix products  62.3 us (29%)
  blocking collectives  49.5 us (23%)
  between operations  14.1 us (7%)
  other arithmetic  10 us (5%)
  starting transfers between devices  4.87 us (2%)
    dot_general x8, matrix products, turn(): lax.dot_general(block_h, block_c, (((0,), (0,)), ((), ())), preferred_ele...  55.4 us
    unnamed x4, local copies, waits for them, and re-layouts  38.2 us
    all_gather x1, blocking collectives, per_device(): piece = lax.all_gather(hidden, 'dp', axis=1, tiled=True)  32.4 us
    all_to_all x1, local copies, waits for them, and re-layouts, per_device(): lax.all_to_all(lax.all_to_all(routed[None], 'expert', split_axis=1, conca...  17.1 us
    all_to_all x1, blocking collectives, per_device(): lax.all_to_all(routed[None], 'expert', split_axis=1, concat_axis=1, tiled...  17.1 us
    all_to_all x1, local copies, waits for them, and re-layouts, per_device(): lax.all_to_all(routed[None], 'expert', split_axis=1, concat_axis=1, tiled...  14.6 us
    broadcast_in_dim x1, other arithmetic, per_device(): fisher = (fisher_sum * (1.0 / (ways * groups_dev)))[None]  6.6 us
    all_to_all x1, starting transfers between devices, per_device(): lax.all_to_all(lax.all_to_all(routed[None], 'expert', split_axis=1, conca...  4.87 us
  transfers between devices with their start and end apart: 2, of which 0 were waited for; matrix products, arithmetic and copies ran while one was open for 29% of the time, Pallas kernels for 0%

commit v1 on v0

--- a/solution.py
+++ b/solution.py
@@ -4,6 +4,29 @@
 from jax.sharding import PartitionSpec as P
 
 GROUP = 128
+
+
+def cut_along(array, dim, devices):
+    shape = array.shape
+    tiles = array.reshape(*shape[:dim], devices, shape[dim] // devices, *shape[dim + 1 :])
+    return jnp.moveaxis(tiles, dim, 0)
+
+
+def joined_along(blocks, dim):
+    lengths = list(blocks.shape[1:])
+    lengths[dim] *= blocks.shape[0]
+    return jnp.moveaxis(blocks, 0, dim).reshape(lengths)
+
+
+def rotated_exchange(array, axis, split_dim, concat_dim):
+    devices, here = (lax.axis_size(axis), lax.axis_index(axis))
+    blocks = cut_along(array, split_dim, devices)
+    outs = [blocks[here]]
+    for step in range(1, devices):
+        sent = blocks[(here + step) % devices]
+        outs.append(lax.ppermute(sent, axis, [(i, (i + step) % devices) for i in range(devices)]))
+    blocks = jnp.stack(outs)[(here - jnp.arange(devices)) % devices]
+    return joined_along(blocks, concat_dim)
 
 
 def per_device(cotangent, expert_ids, gate_values, hidden, down_weight):
@@ -28,7 +51,7 @@
     )
     routed = (picked * jnp.transpose(slot_gate, (1, 0, 2))[..., None]).astype(jnp.bfloat16)
     columns = lax.all_to_all(
-        lax.all_to_all(routed[None], "expert", split_axis=1, concat_axis=1, tiled=True),
+        rotated_exchange(routed[None], "expert", 1, 1),
         "dp",
         split_axis=4,
         concat_axis=0,

time: 212 us -> 236 us (1.11)
  local copies, waits for them, and re-layouts: 70.2 us -> 96.3 us
  blocking collectives: 49.5 us -> 33.9 us
  waiting for transfers between devices: 0.02 us -> 8.87 us
  starting transfers between devices: 4.87 us -> 9.33 us
    another operation x0 -> x1, local copies, waits for them, and re-layouts: none -> 24.1 us  [joined_along(): return jnp.moveaxis(blocks, 0, dim).reshape(lengths)]
    all_to_all x1 -> x0, blocking collectives: 17.1 us -> none  [per_device(): lax.all_to_all(routed[None], 'expert', split_axis=1, concat_axis=1, tiled...]
    ppermute x0 -> x3, waiting for transfers between devices: none -> 8.84 us  [rotated_exchange(): lax.ppermute(sent, axis, [(i, (i + step) % devices) for i in range(device...]
    ppermute x0 -> x3, starting transfers between devices: none -> 4.46 us  [rotated_exchange(): lax.ppermute(sent, axis, [(i, (i + step) % devices) for i in range(device...]
    unnamed x4 -> x5, local copies, waits for them, and re-layouts: 38.2 us -> 38.3 us
  transfers between devices with their start and end apart: 2 -> 5, of which waited for: 0 -> 3; matrix products, arithmetic and copies ran while one was open for 29% -> 26% of each run, Pallas kernels for 0% -> 0%
where the time goes in v1:
time: 236 us; the launch traced here: 235 us
  local copies, waits for them, and re-layouts  96.3 us (41%)
  matrix products  62.3 us (26%)
  blocking collectives  33.9 us (14%)
  between operations  14.2 us (6%)
  other arithmetic  10.1 us (4%)
  starting transfers between devices  9.33 us (4%)
  waiting for transfers between devices  8.87 us (4%)
    dot_general x8, matrix products, turn(): lax.dot_general(block_h, block_c, (((0,), (0,)), ((), ())), preferred_ele...  55.4 us
    unnamed x5, local copies, waits for them, and re-layouts  38.3 us
    all_gather x1, blocking collectives, per_device(): piece = lax.all_gather(hidden, 'dp', axis=1, tiled=True)  33.9 us
    all_to_all x2, local copies, waits for them, and re-layouts, per_device(): lax.all_to_all(rotated_exchange(routed[None], 'expert', 1, 1), 'dp', spli...  33 us
    another operation x1, local copies, waits for them, and re-layouts, joined_along(): return jnp.moveaxis(blocks, 0, dim).reshape(lengths)  24.1 us
    ppermute x3, waiting for transfers between devices, rotated_exchange(): lax.ppermute(sent, axis, [(i, (i + step) % devices) for i in range(device...  8.84 us
    broadcast_in_dim x1, other arithmetic, per_device(): fisher = (fisher_sum * (1.0 / (ways * groups_dev)))[None]  6.6 us
    all_to_all x1, starting transfers between devices, per_device(): lax.all_to_all(rotated_exchange(routed[None], 'expert', 1, 1), 'dp', spli...  4.87 us
  transfers between devices with their start and end apart: 5, of which 3 were waited for; matrix products, arithmetic and copies ran while one was open for 26% of the time, Pallas kernels for 0%

profile of v1, /device:TPU:0, one launch (start us, length us, event | category | flops | bytes accessed | tf_op | source)
XLA Modules:
  0.0 235.0 jit_solution(10493241282755671862)
XLA Ops:
  7.2 0.7 fusion.9
  7.9 0.1 copy.42
  8.1 0.2 reduce_window_sum.11
  8.3 0.1 copy.43
  8.4 0.7 select_reduce_fusion.1
  9.2 0.1 select_reduce_fusion
  9.3 2.6 %fusion.6 = bf16[4,2,8,7168]{3,2,0,1:T(8,128)(2,1)S(1)} fusion(bf16[2,128,7168,1]{2,1,3,0:T(8,128)(2,1)} %bitcast.62, f32[4,2,8]{2,0,1:T(4,128)S(1)} %bitcast.71, s32[2,128,4]{1,2,0:T(4,128)S(1)} %copy.43, pred[2,128,4]{1,2,0:T(4,128)(4,1)S(1)} %copy.44), kind=kOutput, calls=%fused_computation.9 | convolution fusion | flops 118374400 | bytes 4592896 | tf_op jit(solution)/shard_map/jgec,jgd->ejcd/dot_general | solution.py:49
  11.9 0.1 dynamic-slice_bitcast_fusion.3
  12.0 0.5 collective-permute-start
  12.5 2.6 %collective-permute-start.1 = (bf16[1,1,2,8,7168]{4,3,2,1,0:T(8,128)(2,1)S(1)}, bf16[1,1,2,8,7168]{4,3,2,1,0:T(8,128)(2,1)S(1)}, u32[]{:S(2)}, u32[]{:S(2)}) collective-permute-start(bf16[1,1,2,8,7168]{4,3,2,1,0:T(8,128)(2,1)S(1)} %get-tuple-element.186), channel_id=1, source_target_pairs={{0,8},{4,12},{8,0},{12,4},{1,9},{5,13},{9,1},{13,5},{2,10},{6,14},... | collective-permute-start | bytes 688136 | tf_op jit(solution)/shard_map/ppermute | solution.py:27
  15.1 1.4 collective-permute-start.2
  16.5 3.2 %collective-permute-done = bf16[1,1,2,8,7168]{4,3,2,1,0:T(8,128)(2,1)S(1)} collective-permute-done((bf16[1,1,2,8,7168]{4,3,2,1,0:T(8,128)(2,1)S(1)}, bf16[1,1,2,8,7168]{4,3,2,1,0:T(8,128)(2,1)S(1)}, u32[]{:S(2)}, u32[]{:S(2)}) %collective-permute-start) | collective-permute-done | bytes 229408 | tf_op jit(solution)/shard_map/ppermute | solution.py:27
  19.7 1.8 collective-permute-done.1
  21.5 3.8 %collective-permute-done.2 = bf16[1,1,2,8,7168]{4,3,2,1,0:T(8,128)(2,1)S(1)} collective-permute-done((bf16[1,1,2,8,7168]{4,3,2,1,0:T(8,128)(2,1)S(1)}, bf16[1,1,2,8,7168]{4,3,2,1,0:T(8,128)(2,1)S(1)}, u32[]{:S(2)}, u32[]{:S(2)}) %collective-permute-start.2) | collective-permute-done | bytes 229408 | tf_op jit(solution)/shard_map/ppermute | solution.py:27
  25.3 0.1 maximum_bitcast_fusion
  25.4 0.6 gather_fusion
  26.1 24.1 %copy.45 = bf16[1,4,2,8,7168]{3,2,1,0,4:T(2,128)(2,1)} copy(bf16[1,4,2,8,7168]{4,3,2,1,0:T(8,128)(2,1)S(1)} %bitcast.63) | data formatting | bytes 1835008 | tf_op jit(solution)/shard_map/reshape;transpose | solution.py:18
  50.1 0.0 copy-start
  50.1 18.8 %reshape.150 = bf16[4,2,57344]{2,1,0:T(2,128)(2,1)} reshape(bf16[7168,1,4,2,8]{4,3,2,1,0:T(2,128)(2,1)} %bitcast.58) | data formatting | bytes 1835008
  68.9 4.9 %all-to-all-start = ((bf16[4,2,57344]{2,1,0:T(2,128)(2,1)}), bf16[4,2,57344]{2,1,0:T(2,128)(2,1)S(1)}, u32[]{:S(2)}, u32[]{:S(2)}) async-start(bf16[4,2,57344]{2,1,0:T(2,128)(2,1)} %reshape.150), calls=%async_computation | async-start | bytes 1835008 | tf_op jit(solution)/shard_map/all_to_all | solution.py:53
  73.8 0.0 reduce-scatter.2.cloned.1.call-start
  73.8 0.0 copy-done
  73.8 33.9 %all_gather.3 = bf16[1,4,4,2,8,1024]{5,4,3,2,0,1:T(8,128)(2,1)S(1)} all-gather(bf16[1,1,4,2,8,1024]{5,4,3,2,0,1:T(8,128)(2,1)S(1)} %bitcast.69), channel_id=1, replica_groups=mesh['group'=2,'expert'=4,'dp'=4] {'dp'}, dimensions={1}, use_global_device_ids=true | all-gather | bytes 655360 | tf_op jit(solution)/shard_map/all_gather | solution.py:72
  107.7 0.0 all-to-all-done
  107.7 19.4 %reshape.151 = bf16[7168,1,4,2,8]{4,3,2,1,0:T(2,128)(2,1)} reshape(bf16[4,2,57344]{2,1,0:T(2,128)(2,1)S(1)} %all-to-all-done) | data formatting | bytes 1835008
  127.1 32.9 %copy.51 = bf16[1,4,2,8,4,1792]{5,4,3,2,1,0:T(4,128)(2,1)S(1)} copy(bf16[1,4,2,8,4,1792]{3,2,1,5,4,0:T(2,128)(2,1)} %bitcast.59) | data formatting | bytes 1835008 | tf_op jit(solution)/shard_map/all_to_all | solution.py:53
  160.0 0.1 copy.48
  160.1 0.1 copy.49
  160.2 4.2 %fusion.7 = f32[256,1024]{1,0:T(8,128)} fusion(bf16[256,1792]{1,0:T(8,128)(2,1)S(1)} %bitcast.65, bf16[1,1024,1792]{2,1,0:T(8,128)(2,1)} %param.11), kind=kOutput, calls=%fused_computation.11 | convolution fusion | flops 939524096 | bytes 5636096 | tf_op jit(solution)/shard_map/dot_general | solution.py:62
  164.4 0.0 reduce-scatter.2.cloned.1.call-update
  164.4 55.5 %while.17 = (s32[]{:T(128)}, f32[1024,1792]{1,0:T(8,128)}, bf16[1,4,4,2,8,1024]{5,4,3,2,1,0:T(8,128)(2,1)S(1)}, bf16[4,4,2,8,1792]{4,3,2,1,0:T(8,128)(2,1)S(1)},...) while((s32[]{:T(128)}, f32[1024,1792]{1,0:T(8,128)}, ...), condition=%wide.region_5.6_spmd.clone, body=%wide.region_4.5_spmd.clone.sunk | while | flops 122945560 | bytes 14863173 | solution.py:91
  164.4 4.2 %select_add_fusion.2 = f32[1024,1792]{1,0:T(8,128)} fusion(f32[1024,1792]{1,0:T(8,128)} %get-tuple-element.224, pred[]{:T(512)S(6)} %compare.26, bf16[4,4,2,8,1792]{4,3,2,1,0:T(8,128)(2,1)S(1)} %get-tuple-element.236, s32[]{:T(128)S(6)} %select_n.159, s32[]{:T(128)S(6)} %select_n.162, bf16[1,4,4,2,8,1024]{5,4,3,2,1,0:T(8,128)(2,1)S(1)} %get-tuple-element.235), kind=kOutput, calls=%fused_computation.1.clone.1 | convolution fusion | flops 122945536 | bytes 14862848 | tf_op jit(solution)/shard_map/while/body/eval_jaxpr/dot_general | solution.py:86
  168.6 7.5 %select_add_fusion.2 = f32[1024,1792]{1,0:T(8,128)} fusion(f32[1024,1792]{1,0:T(8,128)} %get-tuple-element.224, pred[]{:T(512)S(6)} %compare.26, bf16[4,4,2,8,1792]{4,3,2,1,0:T(8,128)(2,1)S(1)} %get-tuple-element.236, s32[]{:T(128)S(6)} %select_n.159, s32[]{:T(128)S(6)} %select_n.162, bf16[1,4,4,2,8,1024]{5,4,3,2,1,0:T(8,128)(2,1)S(1)} %get-tuple-element.235), kind=kOutput, calls=%fused_computation.1.clone.1 | convolution fusion | flops 122945536 | bytes 14862848 | tf_op jit(solution)/shard_map/while/body/eval_jaxpr/dot_general | solution.py:86
  176.1 7.3 %select_add_fusion.2 = f32[1024,1792]{1,0:T(8,128)} fusion(f32[1024,1792]{1,0:T(8,128)} %get-tuple-element.224, pred[]{:T(512)S(6)} %compare.26, bf16[4,4,2,8,1792]{4,3,2,1,0:T(8,128)(2,1)S(1)} %get-tuple-element.236, s32[]{:T(128)S(6)} %select_n.159, s32[]{:T(128)S(6)} %select_n.162, bf16[1,4,4,2,8,1024]{5,4,3,2,1,0:T(8,128)(2,1)S(1)} %get-tuple-element.235), kind=kOutput, calls=%fused_computation.1.clone.1 | convolution fusion | flops 122945536 | bytes 14862848 | tf_op jit(solution)/shard_map/while/body/eval_jaxpr/dot_general | solution.py:86
  183.4 7.3 %select_add_fusion.2 = f32[1024,1792]{1,0:T(8,128)} fusion(f32[1024,1792]{1,0:T(8,128)} %get-tuple-element.224, pred[]{:T(512)S(6)} %compare.26, bf16[4,4,2,8,1792]{4,3,2,1,0:T(8,128)(2,1)S(1)} %get-tuple-element.236, s32[]{:T(128)S(6)} %select_n.159, s32[]{:T(128)S(6)} %select_n.162, bf16[1,4,4,2,8,1024]{5,4,3,2,1,0:T(8,128)(2,1)S(1)} %get-tuple-element.235), kind=kOutput, calls=%fused_computation.1.clone.1 | convolution fusion | flops 122945536 | bytes 14862848 | tf_op jit(solution)/shard_map/while/body/eval_jaxpr/dot_general | solution.py:86
  190.7 7.3 %select_add_fusion.2 = f32[1024,1792]{1,0:T(8,128)} fusion(f32[1024,1792]{1,0:T(8,128)} %get-tuple-element.224, pred[]{:T(512)S(6)} %compare.26, bf16[4,4,2,8,1792]{4,3,2,1,0:T(8,128)(2,1)S(1)} %get-tuple-element.236, s32[]{:T(128)S(6)} %select_n.159, s32[]{:T(128)S(6)} %select_n.162, bf16[1,4,4,2,8,1024]{5,4,3,2,1,0:T(8,128)(2,1)S(1)} %get-tuple-element.235), kind=kOutput, calls=%fused_computation.1.clone.1 | convolution fusion | flops 122945536 | bytes 14862848 | tf_op jit(solution)/shard_map/while/body/eval_jaxpr/dot_general | solution.py:86
  198.1 7.3 %select_add_fusion.2 = f32[1024,1792]{1,0:T(8,128)} fusion(f32[1024,1792]{1,0:T(8,128)} %get-tuple-element.224, pred[]{:T(512)S(6)} %compare.26, bf16[4,4,2,8,1792]{4,3,2,1,0:T(8,128)(2,1)S(1)} %get-tuple-element.236, s32[]{:T(128)S(6)} %select_n.159, s32[]{:T(128)S(6)} %select_n.162, bf16[1,4,4,2,8,1024]{5,4,3,2,1,0:T(8,128)(2,1)S(1)} %get-tuple-element.235), kind=kOutput, calls=%fused_computation.1.clone.1 | convolution fusion | flops 122945536 | bytes 14862848 | tf_op jit(solution)/shard_map/while/body/eval_jaxpr/dot_general | solution.py:86
  205.3 7.3 %select_add_fusion.2 = f32[1024,1792]{1,0:T(8,128)} fusion(f32[1024,1792]{1,0:T(8,128)} %get-tuple-element.224, pred[]{:T(512)S(6)} %compare.26, bf16[4,4,2,8,1792]{4,3,2,1,0:T(8,128)(2,1)S(1)} %get-tuple-element.236, s32[]{:T(128)S(6)} %select_n.159, s32[]{:T(128)S(6)} %select_n.162, bf16[1,4,4,2,8,1024]{5,4,3,2,1,0:T(8,128)(2,1)S(1)} %get-tuple-element.235), kind=kOutput, calls=%fused_computation.1.clone.1 | convolution fusion | flops 122945536 | bytes 14862848 | tf_op jit(solution)/shard_map/while/body/eval_jaxpr/dot_general | solution.py:86
  212.6 7.3 %select_add_fusion.2 = f32[1024,1792]{1,0:T(8,128)} fusion(f32[1024,1792]{1,0:T(8,128)} %get-tuple-element.224, pred[]{:T(512)S(6)} %compare.26, bf16[4,4,2,8,1792]{4,3,2,1,0:T(8,128)(2,1)S(1)} %get-tuple-element.236, s32[]{:T(128)S(6)} %select_n.159, s32[]{:T(128)S(6)} %select_n.162, bf16[1,4,4,2,8,1024]{5,4,3,2,1,0:T(8,128)(2,1)S(1)} %get-tuple-element.235), kind=kOutput, calls=%fused_computation.1.clone.1 | convolution fusion | flops 122945536 | bytes 14862848 | tf_op jit(solution)/shard_map/while/body/eval_jaxpr/dot_general | solution.py:86
  219.9 6.6 %multiply_bitcast_fusion = f32[1,1024,1792]{2,1,0:T(8,128)} fusion(f32[1024,1792]{1,0:T(8,128)} %get-tuple-element.140), kind=kLoop, calls=%fused_computation.10 | loop fusion | flops 1835008 | bytes 14680064 | tf_op jit(solution)/shard_map/broadcast_in_dim | solution.py:92
  226.5 0.0 reduce-scatter.2.cloned.1.call-done
  226.5 1.6 convert_element_type.26
  (8 shorter events, 0.1 us)
Async XLA Ops:
  12.0 7.7 %collective-permute-start = (bf16[1,1,2,8,7168]{4,3,2,1,0:T(8,128)(2,1)S(1)}, bf16[1,1,2,8,7168]{4,3,2,1,0:T(8,128)(2,1)S(1)}, u32[]{:S(2)}, u32[]{:S(2)}) collective-permute-start(bf16[1,1,2,8,7168]{4,3,2,1,0:T(8,128)(2,1)S(1)} %get-tuple-element.187), channel_id=1, source_target_pairs={{0,4},{4,8},{8,12},{12,0},{1,5},{5,9},{9,13},{13,1},{2,6},{6,10},{... | collective-permute-start | bytes 688136 | tf_op jit(solution)/shard_map/ppermute | solution.py:27
  12.5 9.0 %collective-permute-start.1 = (bf16[1,1,2,8,7168]{4,3,2,1,0:T(8,128)(2,1)S(1)}, bf16[1,1,2,8,7168]{4,3,2,1,0:T(8,128)(2,1)S(1)}, u32[]{:S(2)}, u32[]{:S(2)}) collective-permute-start(bf16[1,1,2,8,7168]{4,3,2,1,0:T(8,128)(2,1)S(1)} %get-tuple-element.186), channel_id=1, source_target_pairs={{0,8},{4,12},{8,0},{12,4},{1,9},{5,13},{9,1},{13,5},{2,10},{6,14},... | collective-permute-start | bytes 688136 | tf_op jit(solution)/shard_map/ppermute | solution.py:27
  15.1 10.3 %collective-permute-start.2 = (bf16[1,1,2,8,7168]{4,3,2,1,0:T(8,128)(2,1)S(1)}, bf16[1,1,2,8,7168]{4,3,2,1,0:T(8,128)(2,1)S(1)}, u32[]{:S(2)}, u32[]{:S(2)}) collective-permute-start(bf16[1,1,2,8,7168]{4,3,2,1,0:T(8,128)(2,1)S(1)} %get-tuple-element.185), channel_id=1, source_target_pairs={{0,12},{4,0},{8,4},{12,8},{1,13},{5,1},{9,5},{13,9},{2,14},{6,2},{... | collective-permute-start | bytes 688136 | tf_op jit(solution)/shard_map/ppermute | solution.py:27
  50.1 23.7 %copy-start = (bf16[1,1,4,2,8,1024]{5,4,3,2,1,0:T(8,128)(2,1)S(1)}, bf16[1,1,4,2,8,1024]{5,4,3,2,1,0:T(8,128)(2,1)}, u32[]{:S(2)}) copy-start(bf16[1,1,4,2,8,1024]{5,4,3,2,1,0:T(8,128)(2,1)} %param.10) | copy-start | bytes 393220
  68.9 38.8 %all-to-all-start = ((bf16[4,2,57344]{2,1,0:T(2,128)(2,1)}), bf16[4,2,57344]{2,1,0:T(2,128)(2,1)S(1)}, u32[]{:S(2)}, u32[]{:S(2)}) async-start(bf16[4,2,57344]{2,1,0:T(2,128)(2,1)} %reshape.150), calls=%async_computation | async-start | bytes 1835008 | tf_op jit(solution)/shard_map/all_to_all | solution.py:53
  73.8 152.7 %reduce-scatter.2.cloned.1.call-start = ((), (), s32[]{:S(2)}) async-start(), calls=%async_computation.2 | async-start | bytes 1310720 | tf_op jit(solution)/shard_map/reduce_scatter | solution.py:61
Sparse Core Ops, SparseCore 0:
  164.5 27.2 reduce-scatter.1
